TPU v7x, 32 devices: a whole 2x2x4 slice. The times are simulated.
32 devices in a mesh: tick: 16 (over z, y, x), wire: 2 (over core).
Axes of the slice: x: 2, y: 2, z: 4, core: 2. Of those that a mesh axis runs over, the one named last changes fastest.
Arguments:
- trigger: bfloat16 [2048, 16, 1280], P('tick', None, 'wire'), may hold values from -6 to 6
- response: float32 [2, 21, 1024], replicated, may hold values from -1.2 to 1.2
- wiener: float32 [1024], replicated, may hold values from 0.2 to 2
- roi_mask: int32 [16, 1280, 16], P('tick', 'wire'), may hold values 0 or 1
- cell_map: int32 [16, 1280], P('tick', 'wire'), may hold values from 0 to 127, as said below
Outputs:
- signal: bfloat16 [16, 1280, 2048], P('tick', 'wire')
- cell_charge: float32 [128, 2048], P('tick', 'wire')
Inputs may be any that keep to these rules, and one draw needn't show every extreme that they name: `cell_map`: A channel's cell c belongs to owner c // 8. Among the 640 channels of one device (an aligned block of 640 wires of one plane), at most 80 name cells of one owner; in every draw some owner gets exactly 80 channels from every such block.
All inputs are finite; a program needn't handle non-finite values. No bound on the sum of `roi_mask` on one device may be relied on, other than what follows from the above.
Results may differ from a plain program's by a relative error of at most 0.008.
Values may be sent and summed in bfloat16 or wider, within the bound.
A program may use at most 128 MiB of HBM per device.

v0:
```python
import math
import jax
import jax.numpy as jnp
from jax import lax
from jax.sharding import PartitionSpec as P

TICKS = 2048
RESP_TAPS = 21
ROI_TICKS = 128
CELLS_OWN = 8
FREQS = 1024
HALO = 10
charge_scale = 0.1


def with_halo(cells, sides, width):
    for axis, dim in sides:
        count = lax.axis_size(axis)
        ends = count - 1
        head = lax.slice_in_dim(cells, 0, width, axis=dim)
        tail = lax.slice_in_dim(cells, cells.shape[dim] - width, cells.shape[dim], axis=dim)
        cells = jnp.concatenate(
            [
                lax.ppermute(tail, axis, [(i, (i + 1) % count) for i in range(ends)]),
                cells,
                lax.ppermute(head, axis, [((i + 1) % count, i) for i in range(ends)]),
            ],
            axis=dim,
        )
    return cells


def build_tables():
    frequency = jnp.arange(FREQS, dtype=jnp.int32)
    tick_index = jnp.arange(TICKS, dtype=jnp.int32)
    phase_angle = (frequency[:, None] * tick_index[None, :] % TICKS).astype(jnp.float32) * (
        2.0 * math.pi / TICKS
    )
    cosine = jnp.cos(phase_angle).astype(jnp.bfloat16)
    sine_table = jnp.sin(phase_angle).astype(jnp.bfloat16)
    forward = jnp.concatenate([cosine, -sine_table], axis=0)
    weight = jnp.where(frequency == 0, 1.0, 2.0).astype(jnp.bfloat16)[:, None]
    inverse = jnp.concatenate([cosine * weight, -sine_table * weight], axis=0)
    return (forward, inverse)


def transform(forward, waves):
    return (jnp.dot(forward, waves, preferred_element_type=jnp.float32) * TICKS ** (-0.5)).astype(
        jnp.bfloat16
    )


def deconvolve(spectrum, response, wiener, wire_count):
    real_part = spectrum[:FREQS].astype(jnp.float32)
    imag_part = spectrum[FREQS:].astype(jnp.float32)
    sum_real = jnp.zeros((FREQS, wire_count), jnp.float32)
    sum_imag = jnp.zeros((FREQS, wire_count), jnp.float32)
    for offset in range(RESP_TAPS):
        shifted_real = real_part[:, offset : offset + wire_count]
        shifted_imag = imag_part[:, offset : offset + wire_count]
        resp_real = response[0, offset][:, None]
        resp_imag = response[1, offset][:, None]
        sum_real = sum_real + resp_real * shifted_real - resp_imag * shifted_imag
        sum_imag = sum_imag + resp_real * shifted_imag + resp_imag * shifted_real
    gain_column = wiener[:, None]
    return jnp.concatenate([sum_real * gain_column, sum_imag * gain_column], axis=0).astype(
        jnp.bfloat16
    )


def on_device(trigger, response, wiener, roi_mask, cell_map):
    forward, inverse = build_tables()
    wire_count = trigger.shape[2]
    norm_factor = TICKS ** (-0.5)
    local_spectrum = transform(
        forward, lax.all_to_all(trigger, "tick", split_axis=1, concat_axis=0, tiled=True)[:, 0, :]
    )
    spectrum = with_halo(local_spectrum, (("wire", 1),), HALO)
    filtered = deconvolve(spectrum, response, wiener, wire_count)
    unmasked = (
        lax.dot_general(
            filtered, inverse, (((0,), (0,)), ((), ())), preferred_element_type=jnp.float32
        )
        * norm_factor
    )
    blocks = roi_mask[0].astype(jnp.float32)
    signal = (
        (unmasked.reshape(wire_count, -1, ROI_TICKS) * blocks[:, :, None])
        .reshape(wire_count, TICKS)
        .astype(jnp.bfloat16)
    )
    channel_cells = cell_map[0]
    labels = jnp.arange(CELLS_OWN * lax.axis_size("tick"), dtype=jnp.int32)
    selector = (channel_cells[None, :] == labels[:, None]).astype(jnp.bfloat16)
    partial_value = lax.psum_scatter(
        jnp.dot(selector, signal, preferred_element_type=jnp.float32),
        "tick",
        scatter_dimension=0,
        tiled=True,
    )
    halves = lax.psum_scatter(
        partial_value.astype(jnp.bfloat16), "wire", scatter_dimension=1, tiled=True
    ).astype(jnp.float32)
    return (signal[None], halves * charge_scale)


def solution(mesh):
    in_specs = (P("tick", None, "wire"), P(), P(), P("tick", "wire", None), P("tick", "wire"))
    out_specs = (P("tick", "wire", None), P("tick", "wire"))
    return jax.shard_map(
        on_device, mesh=mesh, in_specs=in_specs, out_specs=out_specs, check_vma=False
    )
```

profile of v0, /device:TPU:0, one launch (start us, length us, event | category | flops | bytes accessed | tf_op | source)
XLA Modules:
  0.0 273.0 jit_solution(17339042890176495829)
XLA Ops:
  7.2 3.8 %copy.8 = bf16[128,16,640]{2,0,1:T(8,128)(2,1)} copy(bf16[128,16,640]{2,1,0:T(8,128)(2,1)} %param.5) | data formatting | bytes 5242880 | tf_op args[0]
  11.0 8.5 %all-to-all-start = ((bf16[128,16,640]{2,0,1:T(8,128)(2,1)}), bf16[128,16,640]{2,0,1:T(8,128)(2,1)}, u32[]{:S(2)}, u32[]{:S(2)}) async-start(bf16[128,16,640]{2,0,1:T(8,128)(2,1)} %copy.8), calls=%async_computation | async-start | bytes 5242880 | tf_op jit(solution)/shard_map/all_to_all | solution.py:76
  19.6 0.1 fusion.29
  19.7 31.4 %cosine_convert_fusion = bf16[1024,2048]{1,0:T(8,128)(2,1)} fusion(), kind=kLoop, calls=%fused_computation.15 | loop fusion | flops 31457280 | bytes 4194304 | tf_op jit(solution)/shard_map/convert_element_type | solution.py:39
  51.1 32.0 %fusion.15 = bf16[1024,2048]{1,0:T(8,128)(2,1)} fusion(), kind=kLoop, calls=%fused_computation.22 | loop fusion | flops 37748736 | bytes 4194304 | tf_op jit(solution)/shard_map/neg | solution.py:41
  83.2 35.4 %broadcast_multiply_fusion.1 = (bf16[1024,2048]{1,0:T(8,128)(2,1)}, bf16[1024,2048]{1,0:T(8,128)(2,1)}) fusion(bf16[1024]{0:T(1024)(128)(2,1)S(1)} %select_convert_fusion), kind=kLoop, calls=%fused_computation.30 | loop fusion | flops 50331648 | bytes 8390656 | tf_op jit(solution)/shard_map/mul | solution.py:43
  118.5 9.9 %multiply_convert_fusion = bf16[2048,640]{0,1:T(8,128)(2,1)S(1)} fusion(bf16[2048,640]{1,0:T(8,128)(2,1)} %bitcast.3, bf16[1024,2048]{1,0:T(8,128)(2,1)} %fusion.15, bf16[1024,2048]{1,0:T(8,128)(2,1)} %cosine_convert_fusion), kind=kOutput, calls=%fused_computation.21 | convolution fusion | flops 5388107776 | bytes 13631488 | tf_op jit(solution)/shard_map/dot_general | solution.py:48
  128.4 1.5 collective-permute-start
  129.9 1.5 collective-permute-start.1
  131.4 0.2 copy.9
  131.6 1.4 collective-permute-done.1
  133.1 0.7 pad_maximum_fusion
  133.8 0.7 slice_convert_fusion.1
  134.5 15.2 %multiply_convert_fusion.2 = bf16[1024,640]{0,1:T(8,128)(2,1)} fusion(f32[1024,660]{0,1:T(8,128)S(1)} %get-tuple-element.3, f32[1024,660]{0,1:T(8,128)S(1)} %get-tuple-element.2, f32[1024]{0:T(1024)S(1)} %copy-done.5, f32[1024]{0:T(1024)S(1)} %bitcast.139, f32[1024]{0:T(1024)S(1)} %bitcast.141, f32[1024]{0:T(1024)S(1)} %bitcast.61, f32[1024]{0:T(1024)S(1)} %bitcast.63, ...), kind=kLoop, calls=%fused_computation.28 | loop fusion | flops 55705600 | bytes 111587328 | tf_op jit(solution)/shard_map/convert
  149.7 15.1 %multiply_convert_fusion.1 = bf16[1024,640]{0,1:T(8,128)(2,1)} fusion(f32[1024,660]{0,1:T(8,128)S(1)} %get-tuple-element.3, f32[1024,660]{0,1:T(8,128)S(1)} %get-tuple-element.2, f32[1024]{0:T(1024)S(1)} %copy-done.5, f32[1024]{0:T(1024)S(1)} %bitcast.140, f32[1024]{0:T(1024)S(1)} %bitcast.142, f32[1024]{0:T(1024)S(1)} %bitcast.62, f32[1024]{0:T(1024)S(1)} %bitcast.64, ...), kind=kLoop, calls=%fused_computation.27 | loop fusion | flops 55705600 | bytes 111587328 | tf_op jit(solution)/shard_map/convert.1
  164.8 1.5 mul.957
  166.3 0.7 copy-done
  167.0 0.4 copy-done.2
  167.4 9.8 %fusion.14 = bf16[640,2048]{1,0:T(8,128)(2,1)S(1)} fusion(f32[80,8,16,128]{3,2,1,0:T(8,128)S(1)} %bitcast.57, bf16[1024,2048]{1,0:T(8,128)(2,1)} %get-tuple-element.49, bf16[1024,2048]{1,0:T(8,128)(2,1)S(1)} %copy-done, bf16[1024,640]{0,1:T(8,128)(2,1)} %multiply_convert_fusion.1, bf16[1024,640]{0,1:T(8,128)(2,1)S(1)} %copy-done.2), kind=kOutput, calls=%fused_computation.20 | convolution fusion | flops 5394661376 | bytes 18874368 | tf_op jit(solution)/shard_map/dot_general | solution.py:81
  177.2 1.8 fusion.23
  179.2 78.9 %reduce-scatter.3.cloned.1.call-done = f32[8,2048]{1,0:T(8,128)} async-done(((f32[128,2048]{1,0:T(8,128)}), f32[8,2048]{1,0:T(8,128)}) %reduce-scatter.3.cloned.1.call-update) | async-done | bytes 65552 | tf_op jit(solution)/shard_map/reduce_scatter | solution.py:95
  258.0 1.5 convert_element_type.68
  259.5 5.3 %reduce-scatter.5.cloned.1.call-done = bf16[8,1024]{1,0:T(8,128)(2,1)} async-done(((bf16[8,2048]{1,0:T(8,128)(2,1)}), bf16[8,1024]{1,0:T(8,128)(2,1)}) %reduce-scatter.5.cloned.1.call-update) | async-done | bytes 16400 | tf_op jit(solution)/shard_map/reduce_scatter | solution.py:101
  264.8 1.3 convert_multiply_fusion
  (24 shorter events, 0.3 us)
Async XLA Ops:
  11.0 8.6 %copy-start.4 = (s32[1,640,16]{1,2,0:T(8,128)S(1)}, s32[1,640,16]{1,2,0:T(8,128)}, u32[]{:S(2)}) copy-start(s32[1,640,16]{1,2,0:T(8,128)} %param.8) | copy-start | bytes 122884
  11.0 8.6 %copy-start.3 = (f32[2,21,1024]{2,0,1:T(2,128)S(1)}, f32[2,21,1024]{2,0,1:T(2,128)}, u32[]{:S(2)}) copy-start(f32[2,21,1024]{2,0,1:T(2,128)} %param.6) | copy-start | bytes 516100
  11.0 107.5 %all-to-all-start = ((bf16[128,16,640]{2,0,1:T(8,128)(2,1)}), bf16[128,16,640]{2,0,1:T(8,128)(2,1)}, u32[]{:S(2)}, u32[]{:S(2)}) async-start(bf16[128,16,640]{2,0,1:T(8,128)(2,1)} %copy.8), calls=%async_computation | async-start | bytes 5242880 | tf_op jit(solution)/shard_map/all_to_all | solution.py:76
  19.5 238.5 %reduce-scatter.3.cloned.1.call-start = ((), (), s32[]{:S(2)}) async-start(), calls=%async_computation.3 | async-start | bytes 1114112 | tf_op jit(solution)/shard_map/reduce_scatter | solution.py:95
  118.5 13.1 %copy-start.6 = (s32[1,640]{1,0:T(1,128)S(1)}, s32[1,640]{1,0:T(1,128)}, u32[]{:S(2)}) copy-start(s32[1,640]{1,0:T(1,128)} %param.9) | copy-start | bytes 7684
  128.4 3.2 %collective-permute-start = (bf16[2048,10]{0,1:T(8,128)(2,1)S(1)}, bf16[2048,10]{0,1:T(8,128)(2,1)S(1)}, u32[]{:S(2)}, u32[]{:S(2)}) collective-permute-start(bf16[2048,10]{0,1:T(8,128)(2,1)S(1)} %get-tuple-element.4), channel_id=1, source_target_pairs={{0,1},{2,3},{4,5},{6,7},{8,9},{10,11},{12,13},{14,15},{16,17},{18,... | collective-permute-start | bytes 122888 | tf_op jit(solution)/shard_map/ppermute | solution.py:24
  129.9 3.1 %collective-permute-start.1 = (bf16[2048,10]{0,1:T(8,128)(2,1)S(1)}, bf16[2048,10]{0,1:T(8,128)(2,1)S(1)}, u32[]{:S(2)}, u32[]{:S(2)}) collective-permute-start(bf16[2048,10]{0,1:T(8,128)(2,1)S(1)} %get-tuple-element.5), channel_id=1, source_target_pairs={{1,0},{3,2},{5,4},{7,6},{9,8},{11,10},{13,12},{15,14},{17,16},{19,... | collective-permute-start | bytes 122888 | tf_op jit(solution)/shard_map/ppermute | solution.py:26
  133.8 0.7 copy-start.5
  164.8 2.2 copy-start
  164.8 2.6 copy-start.2
  177.2 88.9 %copy-start.1 = (bf16[640,2048]{1,0:T(8,128)(2,1)}, bf16[640,2048]{1,0:T(8,128)(2,1)S(1)}, u32[]{:S(2)}) copy-start(bf16[640,2048]{1,0:T(8,128)(2,1)S(1)} %fusion.14) | copy-start | bytes 7864324
  179.1 85.7 %reduce-scatter.5.cloned.1.call-start = ((), (), s32[]{:S(2)}) async-start(), calls=%async_computation.4 | async-start | bytes 49152 | tf_op jit(solution)/shard_map/reduce_scatter | solution.py:101
Sparse Core Ops, SparseCore 0:
  179.2 78.7 reduce-scatter.2
  260.9 3.9 reduce-scatter.4
where the time goes:
time: 273 us
  other arithmetic  133 us (49%)
  waiting for transfers between devices  85.6 us (31%)
  matrix products  21.6 us (8%)
  between operations  14.2 us (5%)
  starting transfers between devices  11.5 us (4%)
  local copies, waits for them, and re-layouts  6.73 us (2%)
    reduce_scatter x1, waiting for transfers between devices, on_device(): lax.psum_scatter(jnp.dot(selector, signal, preferred_element_type=jnp.flo...  78.9 us
    mul x1, other arithmetic, build_tables(): inverse = jnp.concatenate([cosine * weight, -sine_table * weight], axis=0)  35.4 us
    neg x1, other arithmetic, build_tables(): forward = jnp.concatenate([cosine, -sine_table], axis=0)  32 us
    convert_element_type x1, other arithmetic, build_tables(): cosine = jnp.cos(phase_angle).astype(jnp.bfloat16)  31.4 us
    another operation x2, other arithmetic  30.3 us
    dot_general x1, matrix products, transform(): jnp.dot(forward, waves, preferred_element_type=jnp.float32)  9.88 us
    dot_general x1, matrix products, on_device(): lax.dot_general(filtered, inverse, (((0,), (0,)), ((), ())), preferred_el...  9.84 us
    all_to_all x1, starting transfers between devices, on_device(): lax.all_to_all(trigger, 'tick', split_axis=1, concat_axis=0, tiled=True)  8.49 us
  transfers between devices with their start and end apart: 5, of which 3 were waited for; matrix products, arithmetic and copies ran while one was open for 36% of the time, Pallas kernels for 0%

commit v1 on v0

--- a/solution.py
+++ b/solution.py
@@ -11,6 +11,18 @@
 FREQS = 1024
 HALO = 10
 charge_scale = 0.1
+
+
+def rotated_exchange(x, axis, split, join):
+    ways, here = (lax.axis_size(axis), lax.axis_index(axis))
+    width = x.shape[split] // ways
+    turned = jnp.roll(x, -here * width, axis=split)
+    got = [lax.slice_in_dim(turned, 0, width, axis=split)]
+    for far in range(1, ways):
+        sent = lax.slice_in_dim(turned, far * width, (far + 1) * width, axis=split)
+        got.append(lax.ppermute(sent, axis, [(d, (d + far) % ways) for d in range(ways)]))
+    line = jnp.concatenate(got[::-1], axis=join)
+    return jnp.roll(line, (here + 1) * got[0].shape[join], axis=join)
 
 
 def with_halo(cells, sides, width):
@@ -72,9 +84,7 @@
     forward, inverse = build_tables()
     wire_count = trigger.shape[2]
     norm_factor = TICKS ** (-0.5)
-    local_spectrum = transform(
-        forward, lax.all_to_all(trigger, "tick", split_axis=1, concat_axis=0, tiled=True)[:, 0, :]
-    )
+    local_spectrum = transform(forward, rotated_exchange(trigger, "tick", 1, 0)[:, 0, :])
     spectrum = with_halo(local_spectrum, (("wire", 1),), HALO)
     filtered = deconvolve(spectrum, response, wiener, wire_count)
     unmasked = (

time: 273 us -> 347 us (1.27)
  local copies, waits for them, and re-layouts: 6.73 us -> 31.9 us
  starting transfers between devices: 11.5 us -> 36.2 us
  waiting for transfers between devices: 85.6 us -> 107 us
    ppermute x0 -> x15, starting transfers between devices: none -> 33.5 us  [rotated_exchange(): lax.ppermute(sent, axis, [(d, (d + far) % ways) for d in range(ways)])]
    ppermute x0 -> x15, waiting for transfers between devices: none -> 27.3 us  [rotated_exchange(): lax.ppermute(sent, axis, [(d, (d + far) % ways) for d in range(ways)])]
    unnamed x15 -> x92, local copies, waits for them, and re-layouts: 4.93 us -> 26 us
    all_to_all x1 -> x0, starting transfers between devices: 8.49 us -> none  [on_device(): lax.all_to_all(trigger, 'tick', split_axis=1, concat_axis=0, tiled=True)]
    reduce_scatter x1, waiting for transfers between devices: 78.9 us -> 73.8 us  [on_device(): lax.psum_scatter(jnp.dot(selector, signal, preferred_element_type=jnp.flo...]
  transfers between devices with their start and end apart: 5 -> 19, of which waited for: 3 -> 7; matrix products, arithmetic and copies ran while one was open for 36% -> 32% of each run, Pallas kernels for 0% -> 0%
where the time goes in v1:
time: 347 us
  other arithmetic  136 us (39%)
  waiting for transfers between devices  107 us (31%)
  starting transfers between devices  36.2 us (10%)
  local copies, waits for them, and re-layouts  31.9 us (9%)
  matrix products  20.6 us (6%)
  between operations  14.6 us (4%)
    reduce_scatter x1, waiting for transfers between devices, on_device(): lax.psum_scatter(jnp.dot(selector, signal, preferred_element_type=jnp.flo...  73.8 us
    mul x1, other arithmetic, build_tables(): inverse = jnp.concatenate([cosine * weight, -sine_table * weight], axis=0)  35.3 us
    ppermute x15, starting transfers between devices, rotated_exchange(): lax.ppermute(sent, axis, [(d, (d + far) % ways) for d in range(ways)])  33.5 us
    neg x1, other arithmetic, build_tables(): forward = jnp.concatenate([cosine, -sine_table], axis=0)  32 us
    convert_element_type x1, other arithmetic, build_tables(): cosine = jnp.cos(phase_angle).astype(jnp.bfloat16)  31.4 us
    another operation x2, other arithmetic  30.3 us
    ppermute x15, waiting for transfers between devices, rotated_exchange(): lax.ppermute(sent, axis, [(d, (d + far) % ways) for d in range(ways)])  27.3 us
    unnamed x92, local copies, waits for them, and re-layouts  26 us
  transfers between devices with their start and end apart: 19, of which 7 were waited for; matrix products, arithmetic and copies ran while one was open for 32% of the time, Pallas kernels for 0%

profile of v1, /device:TPU:0, one launch (start us, length us, event | category | flops | bytes accessed | tf_op | source)
XLA Modules:
  0.0 346.6 jit_solution(948340927077294863)
XLA Ops:
  7.2 3.8 %copy.8 = bf16[128,16,640]{2,0,1:T(8,128)(2,1)} copy(bf16[128,16,640]{2,1,0:T(8,128)(2,1)} %param.5) | data formatting | bytes 5242880 | tf_op args[0]
  11.0 2.8 fusion.20
  15.3 7.0 %collective-permute-start = (bf16[128,1,640]{2,0,1:T(8,128)(2,1)}, bf16[128,1,640]{2,0,1:T(8,128)(2,1)S(1)}, u32[]{:S(2)}, u32[]{:S(2)}) collective-permute-start(bf16[128,1,640]{2,0,1:T(8,128)(2,1)} %get-tuple-element.20), channel_id=1, source_target_pairs={{0,30},{2,0},{4,2},{6,4},{8,6},{10,8},{12,10},{14,12},{16,14},{18,... | collective-permute-start | bytes 491528 | tf_op jit(solution)/shard_map/ppermute | solution.py:23
  24.9 31.4 %cosine_convert_fusion = bf16[1024,2048]{1,0:T(8,128)(2,1)} fusion(), kind=kLoop, calls=%fused_computation.15 | loop fusion | flops 31457280 | bytes 4194304 | tf_op jit(solution)/shard_map/convert_element_type | solution.py:51
  56.4 32.0 %fusion.15 = bf16[1024,2048]{1,0:T(8,128)(2,1)} fusion(), kind=kLoop, calls=%fused_computation.24 | loop fusion | flops 37748736 | bytes 4194304 | tf_op jit(solution)/shard_map/neg | solution.py:53
  89.8 35.3 %broadcast_multiply_fusion.1 = (bf16[1024,2048]{1,0:T(8,128)(2,1)}, bf16[1024,2048]{1,0:T(8,128)(2,1)}) fusion(bf16[1024]{0:T(1024)(128)(2,1)S(1)} %select_convert_fusion), kind=kLoop, calls=%fused_computation.35 | loop fusion | flops 50331648 | bytes 8390656 | tf_op jit(solution)/shard_map/mul | solution.py:55
  125.2 4.5 %collective-permute-start.5 = (bf16[128,1,640]{2,0,1:T(8,128)(2,1)}, bf16[128,1,640]{2,0,1:T(8,128)(2,1)S(1)}, u32[]{:S(2)}, u32[]{:S(2)}) collective-permute-start(bf16[128,1,640]{2,0,1:T(8,128)(2,1)} %get-tuple-element.15), channel_id=1, source_target_pairs={{0,20},{2,22},{4,24},{6,26},{8,28},{10,30},{12,0},{14,2},{16,4},{1... | collective-permute-start | bytes 491528 | tf_op jit(solution)/shard_map/ppermute | solution.py:23
  131.1 1.6 collective-permute-start.7
  133.4 2.5 collective-permute-start.8
  136.6 2.6 collective-permute-start.9
  139.8 4.9 %collective-permute-start.10 = (bf16[128,1,640]{2,0,1:T(8,128)(2,1)}, bf16[128,1,640]{2,0,1:T(8,128)(2,1)S(1)}, u32[]{:S(2)}, u32[]{:S(2)}) collective-permute-start(bf16[128,1,640]{2,0,1:T(8,128)(2,1)} %get-tuple-element.10), channel_id=1, source_target_pairs={{0,10},{2,12},{4,14},{6,16},{8,18},{10,20},{12,22},{14,24},{16,26}... | collective-permute-start | bytes 491528 | tf_op jit(solution)/shard_map/ppermute | solution.py:23
  145.4 7.8 %collective-permute-start.11 = (bf16[128,1,640]{2,0,1:T(8,128)(2,1)}, bf16[128,1,640]{2,0,1:T(8,128)(2,1)S(1)}, u32[]{:S(2)}, u32[]{:S(2)}) collective-permute-start(bf16[128,1,640]{2,0,1:T(8,128)(2,1)} %get-tuple-element.9), channel_id=1, source_target_pairs={{0,8},{2,10},{4,12},{6,14},{8,16},{10,18},{12,20},{14,22},{16,24},... | collective-permute-start | bytes 491528 | tf_op jit(solution)/shard_map/ppermute | solution.py:23
  153.8 10.5 %collective-permute-done.7 = bf16[128,1,640]{2,0,1:T(8,128)(2,1)S(1)} collective-permute-done((bf16[128,1,640]{2,0,1:T(8,128)(2,1)}, bf16[128,1,640]{2,0,1:T(8,128)(2,1)S(1)}, u32[]{:S(2)}, u32[]{:S(2)}) %collective-permute-start.7) | collective-permute-done | bytes 163872 | tf_op jit(solution)/shard_map/ppermute | solution.py:23
  165.7 11.3 %collective-permute-done.9 = bf16[128,1,640]{2,0,1:T(8,128)(2,1)S(1)} collective-permute-done((bf16[128,1,640]{2,0,1:T(8,128)(2,1)}, bf16[128,1,640]{2,0,1:T(8,128)(2,1)S(1)}, u32[]{:S(2)}, u32[]{:S(2)}) %collective-permute-start.9) | collective-permute-done | bytes 163872 | tf_op jit(solution)/shard_map/ppermute | solution.py:23
  181.5 4.4 %collective-permute-done.14 = bf16[128,1,640]{2,0,1:T(8,128)(2,1)S(1)} collective-permute-done((bf16[128,1,640]{2,0,1:T(8,128)(2,1)S(1)}, bf16[128,1,640]{2,0,1:T(8,128)(2,1)S(1)}, u32[]{:S(2)}, u32[]{:S(2)}) %collective-permute-start.14) | collective-permute-done | bytes 163872 | tf_op jit(solution)/shard_map/ppermute | solution.py:23
  198.1 8.9 %multiply_convert_fusion = bf16[2048,640]{0,1:T(8,128)(2,1)S(1)} fusion(bf16[1024,2048]{1,0:T(8,128)(2,1)} %fusion.15, bf16[1024,2048]{1,0:T(8,128)(2,1)S(1)} %copy-done.1, bf16[4096,1,640]{2,0,1:T(8,128)(2,1)} %slice_dynamic-update-slice_fusion.1, s32[]{:T(128)S(6)} %select_n.49), kind=kOutput, calls=%fused_computation.23 | convolution fusion | flops 5388107776 | bytes 13631492 | tf_op jit(solution)/shard_map/dot_general | solution.py:60
  213.1 15.3 %multiply_convert_fusion.2 = bf16[1024,640]{0,1:T(8,128)(2,1)} fusion(f32[1024,660]{0,1:T(8,128)S(1)} %get-tuple-element.3, f32[1024,660]{0,1:T(8,128)S(1)} %get-tuple-element.2, f32[1024]{0:T(1024)S(1)} %copy-done.28, f32[1024]{0:T(1024)S(1)} %bitcast.136, f32[1024]{0:T(1024)S(1)} %bitcast.138, f32[1024]{0:T(1024)S(1)} %bitcast.58, f32[1024]{0:T(1024)S(1)} %bitcast.60, ...), kind=kLoop, calls=%fused_computation.32 | loop fusion | flops 55705600 | bytes 111587328 | tf_op jit(solution)/shard_map/convert
  228.3 15.1 %multiply_convert_fusion.1 = bf16[1024,640]{0,1:T(8,128)(2,1)} fusion(f32[1024,660]{0,1:T(8,128)S(1)} %get-tuple-element.3, f32[1024,660]{0,1:T(8,128)S(1)} %get-tuple-element.2, f32[1024]{0:T(1024)S(1)} %copy-done.28, f32[1024]{0:T(1024)S(1)} %bitcast.137, f32[1024]{0:T(1024)S(1)} %bitcast.139, f32[1024]{0:T(1024)S(1)} %bitcast.59, f32[1024]{0:T(1024)S(1)} %bitcast.61, ...), kind=kLoop, calls=%fused_computation.31 | loop fusion | flops 55705600 | bytes 111587328 | tf_op jit(solution)/shard_map/convert.1
  243.4 1.5 mul.961
  246.0 9.8 %fusion.14 = bf16[640,2048]{1,0:T(8,128)(2,1)S(1)} fusion(f32[80,8,16,128]{3,2,1,0:T(8,128)S(1)} %bitcast.54, bf16[1024,2048]{1,0:T(8,128)(2,1)} %get-tuple-element.64, bf16[1024,2048]{1,0:T(8,128)(2,1)S(1)} %copy-done, bf16[1024,640]{0,1:T(8,128)(2,1)} %multiply_convert_fusion.1, bf16[1024,640]{0,1:T(8,128)(2,1)S(1)} %copy-done.3), kind=kOutput, calls=%fused_computation.20 | convolution fusion | flops 5394661376 | bytes 18874368 | tf_op jit(solution)/shard_map/dot_general | solution.py:91
  255.8 1.8 fusion.26
  257.8 73.8 %reduce-scatter.3.cloned.1.call-done = f32[8,2048]{1,0:T(8,128)} async-done(((f32[128,2048]{1,0:T(8,128)}), f32[8,2048]{1,0:T(8,128)}) %reduce-scatter.3.cloned.1.call-update) | async-done | bytes 65552 | tf_op jit(solution)/shard_map/reduce_scatter | solution.py:105
  331.6 1.5 convert_element_type.68
  333.1 5.4 %reduce-scatter.5.cloned.1.call-done = bf16[8,1024]{1,0:T(8,128)(2,1)} async-done(((bf16[8,2048]{1,0:T(8,128)(2,1)}), bf16[8,1024]{1,0:T(8,128)(2,1)}) %reduce-scatter.5.cloned.1.call-update) | async-done | bytes 16400 | tf_op jit(solution)/shard_map/reduce_scatter | solution.py:111
  (132 shorter events, 36.5 us)
Async XLA Ops:
  7.2 324.4 %reduce-scatter.3.cloned.1.call-start = ((), (), s32[]{:S(2)}) async-start(), calls=%async_computation.2 | async-start | bytes 1114112 | tf_op jit(solution)/shard_map/reduce_scatter | solution.py:105
  15.3 109.9 %collective-permute-start = (bf16[128,1,640]{2,0,1:T(8,128)(2,1)}, bf16[128,1,640]{2,0,1:T(8,128)(2,1)S(1)}, u32[]{:S(2)}, u32[]{:S(2)}) collective-permute-start(bf16[128,1,640]{2,0,1:T(8,128)(2,1)} %get-tuple-element.20), channel_id=1, source_target_pairs={{0,30},{2,0},{4,2},{6,4},{8,6},{10,8},{12,10},{14,12},{16,14},{18,... | collective-permute-start | bytes 491528 | tf_op jit(solution)/shard_map/ppermute | solution.py:23
  22.3 108.1 %collective-permute-start.1 = (bf16[128,1,640]{2,0,1:T(8,128)(2,1)}, bf16[128,1,640]{2,0,1:T(8,128)(2,1)S(1)}, u32[]{:S(2)}, u32[]{:S(2)}) collective-permute-start(bf16[128,1,640]{2,0,1:T(8,128)(2,1)} %get-tuple-element.19), channel_id=1, source_target_pairs={{0,28},{2,30},{4,0},{6,2},{8,4},{10,6},{12,8},{14,10},{16,12},{18,... | collective-permute-start | bytes 491528 | tf_op jit(solution)/shard_map/ppermute | solution.py:23
  22.8 108.3 %collective-permute-start.2 = (bf16[128,1,640]{2,0,1:T(8,128)(2,1)}, bf16[128,1,640]{2,0,1:T(8,128)(2,1)S(1)}, u32[]{:S(2)}, u32[]{:S(2)}) collective-permute-start(bf16[128,1,640]{2,0,1:T(8,128)(2,1)} %get-tuple-element.18), channel_id=1, source_target_pairs={{0,26},{2,28},{4,30},{6,0},{8,2},{10,4},{12,6},{14,8},{16,10},{18,... | collective-permute-start | bytes 491528 | tf_op jit(solution)/shard_map/ppermute | solution.py:23
  23.2 110.2 %collective-permute-start.3 = (bf16[128,1,640]{2,0,1:T(8,128)(2,1)}, bf16[128,1,640]{2,0,1:T(8,128)(2,1)S(1)}, u32[]{:S(2)}, u32[]{:S(2)}) collective-permute-start(bf16[128,1,640]{2,0,1:T(8,128)(2,1)} %get-tuple-element.17), channel_id=1, source_target_pairs={{0,24},{2,26},{4,28},{6,30},{8,0},{10,2},{12,4},{14,6},{16,8},{18,... | collective-permute-start | bytes 491528 | tf_op jit(solution)/shard_map/ppermute | solution.py:23
  23.6 112.9 %collective-permute-start.4 = (bf16[128,1,640]{2,0,1:T(8,128)(2,1)}, bf16[128,1,640]{2,0,1:T(8,128)(2,1)S(1)}, u32[]{:S(2)}, u32[]{:S(2)}) collective-permute-start(bf16[128,1,640]{2,0,1:T(8,128)(2,1)} %get-tuple-element.16), channel_id=1, source_target_pairs={{0,22},{2,24},{4,26},{6,28},{8,30},{10,0},{12,2},{14,4},{16,6},{18... | collective-permute-start | bytes 491528 | tf_op jit(solution)/shard_map/ppermute | solution.py:23
  56.4 32.0 %copy-start.4 = (f32[2,21,1024]{2,0,1:T(2,128)S(1)}, f32[2,21,1024]{2,0,1:T(2,128)}, u32[]{:S(2)}) copy-start(f32[2,21,1024]{2,0,1:T(2,128)} %param.6) | copy-start | bytes 516100
  89.8 35.4 %copy-start.7 = (s32[1,640,16]{1,2,0:T(8,128)S(1)}, s32[1,640,16]{1,2,0:T(8,128)}, u32[]{:S(2)}) copy-start(s32[1,640,16]{1,2,0:T(8,128)} %param.8) | copy-start | bytes 122884
  125.2 39.8 %copy-start.6 = (bf16[128,1,640]{2,0,1:T(8,128)(2,1)S(1)}, bf16[128,1,640]{2,0,1:T(8,128)(2,1)}, u32[]{:S(2)}) copy-start(bf16[128,1,640]{2,0,1:T(8,128)(2,1)} %get-tuple-element.7) | copy-start | bytes 491524
  125.2 51.8 %copy-start.5 = (bf16[128,1,640]{2,0,1:T(8,128)(2,1)S(1)}, bf16[128,1,640]{2,0,1:T(8,128)(2,1)}, u32[]{:S(2)}) copy-start(bf16[128,1,640]{2,0,1:T(8,128)(2,1)} %get-tuple-element.6) | copy-start | bytes 491524
  125.2 14.6 %collective-permute-start.5 = (bf16[128,1,640]{2,0,1:T(8,128)(2,1)}, bf16[128,1,640]{2,0,1:T(8,128)(2,1)S(1)}, u32[]{:S(2)}, u32[]{:S(2)}) collective-permute-start(bf16[128,1,640]{2,0,1:T(8,128)(2,1)} %get-tuple-element.15), channel_id=1, source_target_pairs={{0,20},{2,22},{4,24},{6,26},{8,28},{10,30},{12,0},{14,2},{16,4},{1... | collective-permute-start | bytes 491528 | tf_op jit(solution)/shard_map/ppermute | solution.py:23
  130.4 14.9 %collective-permute-start.6 = (bf16[128,1,640]{2,0,1:T(8,128)(2,1)}, bf16[128,1,640]{2,0,1:T(8,128)(2,1)S(1)}, u32[]{:S(2)}, u32[]{:S(2)}) collective-permute-start(bf16[128,1,640]{2,0,1:T(8,128)(2,1)} %get-tuple-element.14), channel_id=1, source_target_pairs={{0,18},{2,20},{4,22},{6,24},{8,26},{10,28},{12,30},{14,0},{16,2},{... | collective-permute-start | bytes 491528 | tf_op jit(solution)/shard_map/ppermute | solution.py:23
  131.1 33.2 %collective-permute-start.7 = (bf16[128,1,640]{2,0,1:T(8,128)(2,1)}, bf16[128,1,640]{2,0,1:T(8,128)(2,1)S(1)}, u32[]{:S(2)}, u32[]{:S(2)}) collective-permute-start(bf16[128,1,640]{2,0,1:T(8,128)(2,1)} %get-tuple-element.13), channel_id=1, source_target_pairs={{0,16},{2,18},{4,20},{6,22},{8,24},{10,26},{12,28},{14,30},{16,0},... | collective-permute-start | bytes 491528 | tf_op jit(solution)/shard_map/ppermute | solution.py:23
  133.4 31.6 %collective-permute-start.8 = (bf16[128,1,640]{2,0,1:T(8,128)(2,1)}, bf16[128,1,640]{2,0,1:T(8,128)(2,1)S(1)}, u32[]{:S(2)}, u32[]{:S(2)}) collective-permute-start(bf16[128,1,640]{2,0,1:T(8,128)(2,1)} %get-tuple-element.12), channel_id=1, source_target_pairs={{0,14},{2,16},{4,18},{6,20},{8,22},{10,24},{12,26},{14,28},{16,30}... | collective-permute-start | bytes 491528 | tf_op jit(solution)/shard_map/ppermute | solution.py:23
  136.6 40.4 %collective-permute-start.9 = (bf16[128,1,640]{2,0,1:T(8,128)(2,1)}, bf16[128,1,640]{2,0,1:T(8,128)(2,1)S(1)}, u32[]{:S(2)}, u32[]{:S(2)}) collective-permute-start(bf16[128,1,640]{2,0,1:T(8,128)(2,1)} %get-tuple-element.11), channel_id=1, source_target_pairs={{0,12},{2,14},{4,16},{6,18},{8,20},{10,22},{12,24},{14,26},{16,28}... | collective-permute-start | bytes 491528 | tf_op jit(solution)/shard_map/ppermute | solution.py:23
  139.8 39.0 %collective-permute-start.10 = (bf16[128,1,640]{2,0,1:T(8,128)(2,1)}, bf16[128,1,640]{2,0,1:T(8,128)(2,1)S(1)}, u32[]{:S(2)}, u32[]{:S(2)}) collective-permute-start(bf16[128,1,640]{2,0,1:T(8,128)(2,1)} %get-tuple-element.10), channel_id=1, source_target_pairs={{0,10},{2,12},{4,14},{6,16},{8,18},{10,20},{12,22},{14,24},{16,26}... | collective-permute-start | bytes 491528 | tf_op jit(solution)/shard_map/ppermute | solution.py:23
  145.4 34.1 %collective-permute-start.11 = (bf16[128,1,640]{2,0,1:T(8,128)(2,1)}, bf16[128,1,640]{2,0,1:T(8,128)(2,1)S(1)}, u32[]{:S(2)}, u32[]{:S(2)}) collective-permute-start(bf16[128,1,640]{2,0,1:T(8,128)(2,1)} %get-tuple-element.9), channel_id=1, source_target_pairs={{0,8},{2,10},{4,12},{6,14},{8,16},{10,18},{12,20},{14,22},{16,24},... | collective-permute-start | bytes 491528 | tf_op jit(solution)/shard_map/ppermute | solution.py:23
  164.3 15.8 %collective-permute-start.12 = (bf16[128,1,640]{2,0,1:T(8,128)(2,1)}, bf16[128,1,640]{2,0,1:T(8,128)(2,1)S(1)}, u32[]{:S(2)}, u32[]{:S(2)}) collective-permute-start(bf16[128,1,640]{2,0,1:T(8,128)(2,1)} %get-tuple-element.8), channel_id=1, source_target_pairs={{0,6},{2,8},{4,10},{6,12},{8,14},{10,16},{12,18},{14,20},{16,22},{... | collective-permute-start | bytes 491528 | tf_op jit(solution)/shard_map/ppermute | solution.py:23
  165.0 15.8 %collective-permute-start.13 = (bf16[128,1,640]{2,0,1:T(8,128)(2,1)S(1)}, bf16[128,1,640]{2,0,1:T(8,128)(2,1)S(1)}, u32[]{:S(2)}, u32[]{:S(2)}) collective-permute-start(bf16[128,1,640]{2,0,1:T(8,128)(2,1)S(1)} %copy-done.6), channel_id=1, source_target_pairs={{0,4},{2,6},{4,8},{6,10},{8,12},{10,14},{12,16},{14,18},{16,20},{1... | collective-permute-start | bytes 491528 | tf_op jit(solution)/shard_map/ppermute | solution.py:23
  177.0 8.9 %collective-permute-start.14 = (bf16[128,1,640]{2,0,1:T(8,128)(2,1)S(1)}, bf16[128,1,640]{2,0,1:T(8,128)(2,1)S(1)}, u32[]{:S(2)}, u32[]{:S(2)}) collective-permute-start(bf16[128,1,640]{2,0,1:T(8,128)(2,1)S(1)} %copy-done.5), channel_id=1, source_target_pairs={{0,2},{2,4},{4,6},{6,8},{8,10},{10,12},{12,14},{14,16},{16,18},{18... | collective-permute-start | bytes 491528 | tf_op jit(solution)/shard_map/ppermute | solution.py:23
  207.0 3.6 %collective-permute-start.15 = (bf16[2048,10]{0,1:T(8,128)(2,1)S(1)}, bf16[2048,10]{0,1:T(8,128)(2,1)S(1)}, u32[]{:S(2)}, u32[]{:S(2)}) collective-permute-start(bf16[2048,10]{0,1:T(8,128)(2,1)S(1)} %get-tuple-element.4), channel_id=1, source_target_pairs={{0,1},{2,3},{4,5},{6,7},{8,9},{10,11},{12,13},{14,15},{16,17},{18,... | collective-permute-start | bytes 122888 | tf_op jit(solution)/shard_map/ppermute | solution.py:36
  208.3 3.1 collective-permute-start.16
  255.8 84.0 %copy-start.2 = (bf16[640,2048]{1,0:T(8,128)(2,1)}, bf16[640,2048]{1,0:T(8,128)(2,1)S(1)}, u32[]{:S(2)}) copy-start(bf16[640,2048]{1,0:T(8,128)(2,1)S(1)} %fusion.14) | copy-start | bytes 7864324
  257.7 80.7 %reduce-scatter.5.cloned.1.call-start = ((), (), s32[]{:S(2)}) async-start(), calls=%async_computation.3 | async-start | bytes 49152 | tf_op jit(solution)/shard_map/reduce_scatter | solution.py:111
  (25 other events, 42.9 us)
Sparse Core Ops, SparseCore 0:
  257.8 73.7 reduce-scatter.2
  334.4 3.9 reduce-scatter.4
